TPU v7x, 512 devices: a whole 4x8x8 slice. The times are simulated.
512 devices in a mesh: hours: 64 (over z, x, core), region: 8 (over y).
Axes of the slice: x: 4, y: 8, z: 8, core: 2. Of those that a mesh axis runs over, the one named last changes fastest.
Arguments:
- availability: float32 [4096, 16, 1024], P('hours', None, 'region'), may hold values from 0.1 to 1
- demand: float32 [4096, 1024], P('hours', 'region'), may hold values from 2 to 72, as said below
- gen_cost: float32 [16, 1024], P(None, 'region'), may hold values from 0.05 to 1
- cap_cost: float32 [8, 2048], P('region', 'hours'), may hold values from 204.8 to 2048
- owner_map: int32 [8, 2048], P('region'), may hold values from 0 to 2047, each once within a row
- line_ends: int32 [2, 2048], P(None, 'region'), may hold values from 0 to 127
- line_limit: float32 [2048], P('region'), may hold values from 0.5 to 4
- cross_ends: int32 [2, 8, 256], P(None, 'region'), may hold values from 0 to 127
- cross_limit: float32 [8, 256], P('region'), may hold values from 0.5 to 4
- pair_counts: int32 [8, 8], P('region'), may hold values from 0 to 32, as said below
- store_node: int32 [2048], P('region'), may hold values from 0 to 127
- store_energy: float32 [2048], P('region'), may hold values from 0.02 to 0.4
- store_power: float32 [2048], P('region'), may hold values from 0.2 to 2
- price_start: float32 [4096, 1024], P('hours', 'region'), may hold values from -3 to 0.5
Outputs:
- dispatch: float32 [4096, 16, 1024], P('hours', None, 'region')
- capacity: float32 [8, 2048], P('region', 'hours')
- prices: float32 [4096, 1024], P('hours', 'region')
- charge_state: float32 [4096, 2048], P('hours', 'region')
Inputs may be any that keep to these rules, and one draw needn't show every extreme that they name: `demand`: loads are positive. `owner_map`: each row lists every capacity column of its region once. `pair_counts`: cross lines in use among the 32 slots of each ordered pair of regions; a region has none to itself; some pair uses all 32.
All inputs are finite; a program needn't handle non-finite values.
Results may differ from a plain program's by a relative error of at most 0.00018.
Values sent between devices are 32-bit elements; how exact they have to be, the bound alone decides.
A program may use at most 64 MiB of HBM per device.

v0:
```python
import jax
import jax.numpy as jnp
from jax import lax
from jax.sharding import PartitionSpec as P

ITERS = 4
epsilon = 1e-06
highest = lax.Precision.HIGHEST


def shifted(value, axis, steps):
    count = lax.axis_size(axis)
    pairs = [(source, (source + steps) % count) for source in range(count)]
    return lax.ppermute(value, axis, pairs)


def one_hot(indices, labels):
    return (indices[:, None] == labels[None, :]).astype(jnp.float32)


def to_owners(partial_value, owned_cols):
    summed = lax.psum(partial_value, "hours")
    return lax.dynamic_slice_in_dim(summed, lax.axis_index("hours") * owned_cols, owned_cols)


def spread_columns(capacity_bar):
    return lax.all_gather(capacity_bar, "hours", axis=0, tiled=True)


def body(
    availability,
    demand,
    gen_cost,
    cap_cost,
    owner_map,
    line_ends,
    line_limit,
    cross_ends,
    cross_limit,
    pair_counts,
    store_node,
    store_energy,
    store_power,
    price_start,
):
    hour_rows, tech_count, node_count = availability.shape
    region_count = lax.axis_size("region")
    slot_count = cross_limit.shape[1]
    slot_width = slot_count // region_count
    owned_cols = cap_cost.shape[1]
    owner_cols = owner_map[0]
    inverse = jnp.argsort(owner_cols)
    node_ids = jnp.arange(node_count, dtype=jnp.int32)
    line_inc = one_hot(line_ends[1], node_ids) - one_hot(line_ends[0], node_ids)
    store_map = one_hot(store_node, node_ids)
    leave_map = one_hot(cross_ends[0, 0], node_ids)
    slot_ids = jnp.arange(slot_count, dtype=jnp.int32)
    pair_of = slot_ids // slot_width
    region_ids = jnp.arange(region_count, dtype=jnp.int32)
    in_use = jnp.sum(
        jnp.where(pair_of[:, None] == region_ids[None, :], pair_counts[0][None, :], 0), axis=1
    )
    cross_bound = jnp.where(slot_ids % slot_width < in_use, cross_limit[0], 0.0)
    reach_map = one_hot(
        pair_of * node_count + cross_ends[1, 0],
        jnp.arange(region_count * node_count, dtype=jnp.int32),
    )
    column_costs = cap_cost[0]
    col_weight = to_owners(jnp.sum(availability, axis=0).reshape(-1)[owner_cols], owned_cols)
    dispatch = jnp.zeros_like(availability)
    capacity = jnp.zeros((owned_cols,), jnp.float32)
    inner_flow = jnp.zeros((hour_rows, line_limit.shape[0]), jnp.float32)
    cross_flow = jnp.zeros((hour_rows, slot_count), jnp.float32)
    mirror_flow = jnp.zeros((hour_rows, slot_count), jnp.float32)
    discharge = jnp.zeros((hour_rows, store_node.shape[0]), jnp.float32)
    charge = jnp.zeros((hour_rows, store_node.shape[0]), jnp.float32)
    prices = price_start
    cap_duals = jnp.zeros_like(availability)
    store_duals = jnp.zeros((hour_rows, store_node.shape[0]), jnp.float32)
    weight = jnp.float32(1.0)
    for iteration in range(ITERS):
        final_sweep = iteration == ITERS - 1
        primal_step = 0.5 / weight
        far_side = jnp.dot(
            lax.all_gather(prices, "region", axis=1, tiled=True), reach_map.T, precision=highest
        )
        if iteration == 0:
            next_duals = jnp.zeros_like(store_duals)
            cap_pull = jnp.zeros((owned_cols,), jnp.float32)
        else:
            next_row = shifted(store_duals[:1], "hours", -1)
            next_duals = jnp.concatenate([store_duals[1:], next_row], axis=0)
            cap_pull = to_owners(
                jnp.sum(availability * cap_duals, axis=0).reshape(-1)[owner_cols], owned_cols
            )
        dispatch_new = jnp.maximum(
            dispatch - primal_step * (gen_cost[None] + prices[:, None, :] + cap_duals), 0.0
        )
        capacity_new = jnp.maximum(
            capacity - (column_costs - cap_pull) / (weight * col_weight), 0.0
        )
        inner_new = jnp.clip(
            inner_flow - primal_step * jnp.dot(prices, line_inc.T, precision=highest),
            -line_limit,
            line_limit,
        )
        cross_new = jnp.clip(
            cross_flow - primal_step * (far_side - jnp.dot(prices, leave_map.T, precision=highest)),
            -cross_bound,
            cross_bound,
        )
        mirror_new = mirror_flow
        discharge_new = jnp.clip(
            discharge
            - primal_step * (jnp.dot(prices, store_map.T, precision=highest) + store_duals),
            -store_power,
            store_power,
        )
        charge_new = jnp.clip(charge - primal_step * (store_duals - next_duals), 0.0, store_energy)
        if not final_sweep:
            cap_change = capacity_new - capacity
            primal_sq = (
                jnp.sum((dispatch_new - dispatch) ** 2)
                + jnp.sum(cap_change**2)
                + jnp.sum((inner_new - inner_flow) ** 2)
                + jnp.sum((cross_new - cross_flow) ** 2)
                + jnp.sum((discharge_new - discharge) ** 2)
                + jnp.sum((charge_new - charge) ** 2)
            )
            primal_sum = lax.psum(primal_sq, ("hours", "region"))
        dispatch_bar = 2.0 * dispatch_new - dispatch
        capacity_bar = 2.0 * capacity_new - capacity
        inner_bar = 2.0 * inner_new - inner_flow
        cross_bar = 2.0 * cross_new - cross_flow
        discharge_bar = 2.0 * discharge_new - discharge
        charge_bar = 2.0 * charge_new - charge
        capacity_all = spread_columns(capacity_bar)
        cap_dense = capacity_all[inverse].reshape(tech_count, node_count)
        per_dest = jnp.dot(cross_bar, reach_map, precision=highest)
        balance = (
            jnp.sum(dispatch_bar, axis=1)
            + jnp.dot(inner_bar, line_inc, precision=highest)
            + (
                lax.psum_scatter(per_dest, "region", scatter_dimension=1, tiled=True)
                - jnp.dot(cross_bar, leave_map, precision=highest)
            )
            + jnp.dot(discharge_bar, store_map, precision=highest)
            - demand
        )
        prev_row = shifted(charge_bar[-1:], "hours", 1)
        storage_rows = (
            charge_bar - jnp.concatenate([prev_row, charge_bar[:-1]], axis=0) + discharge_bar
        )
        cap_rows = dispatch_bar - availability * cap_dense[None]
        prices_new = prices + weight / (tech_count + 8.0) * balance
        cap_new = jnp.maximum(cap_duals + weight / 2.0 * cap_rows, 0.0)
        store_new = store_duals + weight / 3.0 * storage_rows
        if not final_sweep:
            dual_sq = (
                jnp.sum((prices_new - prices) ** 2)
                + jnp.sum((cap_new - cap_duals) ** 2)
                + jnp.sum((store_new - store_duals) ** 2)
            )
            dual_sum = lax.psum(dual_sq, ("hours", "region"))
            weight = jnp.sqrt(weight * jnp.sqrt((dual_sum + epsilon) / (primal_sum + epsilon)))
        dispatch, capacity, inner_flow, cross_flow = (
            dispatch_new,
            capacity_new,
            inner_new,
            cross_new,
        )
        mirror_flow = mirror_new
        discharge, charge = (discharge_new, charge_new)
        prices, cap_duals, store_duals = (prices_new, cap_new, store_new)
    return (dispatch, capacity[None], prices, charge)


def solution(mesh):
    placed = (
        P("hours", None, "region"),
        P("hours", "region"),
        P(None, "region"),
        P("region", "hours"),
        P("region", None),
        P(None, "region"),
        P("region"),
        P(None, "region", None),
        P("region", None),
        P("region", None),
        P("region"),
        P("region"),
        P("region"),
        P("hours", "region"),
    )
    return jax.shard_map(
        body,
        mesh=mesh,
        in_specs=placed,
        out_specs=(
            P("hours", None, "region"),
            P("region", "hours"),
            P("hours", "region"),
            P("hours", "region"),
        ),
        check_vma=False,
    )
```

profile of v0, /device:TPU:2, one launch (start us, length us, event | category | flops | bytes accessed | tf_op | source)
XLA Modules:
  0.0 1496.5 jit_solution(16780039333863139814)
XLA Ops:
  10.0 26.6 %all_gather.21 = f32[64,1024]{1,0:T(8,128)S(1)} all-gather(f32[64,128]{1,0:T(8,128)} %param.27), channel_id=1, replica_groups=mesh['hours'=64,'region'=8] {'region'}, dimensions={1}, use_global_device_ids=true | all-gather | bytes 294912 | tf_op jit(solution)/shard_map/all_gather | solution.py:85
  41.2 11.8 gather_fusion
  53.0 126.8 %psum.70 = f32[2048]{0:T(1024)S(1)} all-reduce(f32[2048]{0:T(1024)S(1)} %gather_fusion), channel_id=1, replica_groups=mesh['hours'=64,'region'=8] {'hours'}, use_global_device_ids=true, to_apply=%region_5.6 | all-reduce | flops 2048 | bytes 16384 | tf_op jit(solution)/shard_map/psum | solution.py:22
  182.5 126.4 %all-reduce = f32[2048]{0:T(1024)S(1)} all-reduce(f32[2048]{0:T(1024)S(1)} %multiply_dynamic-update-slice_fusion), channel_id=1, replica_groups=mesh['hours'=64,'region'=8] {'hours'}, use_global_device_ids=true, to_apply=%add | all-reduce | flops 2048 | bytes 16384
  308.9 5.0 sort.17
  314.0 11.8 gather_fusion.1
  326.8 11.8 gather_fusion.2
  340.6 126.1 %psum.73 = f32[2048]{0:T(1024)S(1)} all-reduce(f32[2048]{0:T(1024)S(1)} %gather_fusion.2), channel_id=1, replica_groups=mesh['hours'=64,'region'=8] {'hours'}, use_global_device_ids=true, to_apply=%region_21.22 | all-reduce | flops 2048 | bytes 16384 | tf_op jit(solution)/shard_map/psum | solution.py:22
  476.0 7.0 collective-permute-start.1
  483.0 95.3 %all-reduce.5 = (f32[]{:T(128)}, f32[]{:T(128)}) all-reduce(f32[]{:T(128)S(6)} %add.309, f32[]{:T(128)S(6)} %add.315), channel_id=1, replica_groups=mesh['hours'=64,'region'=8] {'hours','region'}, use_global_device_ids=true, to_apply=%region_9.10 | all-reduce | flops 2 | bytes 16 | tf_op jit(solution)/shard_map/psum | solution.py:164
  579.7 24.8 %all_gather.23 = f32[64,1024]{1,0:T(8,128)S(1)} all-gather(f32[64,128]{1,0:T(8,128)S(1)} %get-tuple-element.56), channel_id=1, replica_groups=mesh['hours'=64,'region'=8] {'region'}, dimensions={1}, use_global_device_ids=true | all-gather | bytes 294912 | tf_op jit(solution)/shard_map/all_gather | solution.py:85
  606.4 120.4 %all-reduce.1 = f32[2048]{0:T(1024)S(1)} all-reduce(f32[2048]{0:T(1024)S(1)} %subtract_dynamic-update-slice_fusion.1), channel_id=1, replica_groups=mesh['hours'=64,'region'=8] {'hours'}, use_global_device_ids=true, to_apply=%add.1 | all-reduce | flops 2048 | bytes 16384
  726.8 11.8 gather_fusion.3
  744.2 11.8 gather_fusion.4
  758.2 131.1 %psum.76 = f32[2048]{0:T(1024)S(1)} all-reduce(f32[2048]{0:T(1024)S(1)} %gather_fusion.4), channel_id=1, replica_groups=mesh['hours'=64,'region'=8] {'hours'}, use_global_device_ids=true, to_apply=%region_36.37 | all-reduce | flops 2048 | bytes 16384 | tf_op jit(solution)/shard_map/psum | solution.py:22
  900.0 100.8 %all-reduce.4 = (f32[]{:T(128)}, f32[]{:T(128)}) all-reduce(f32[]{:T(128)S(6)} %add.329, f32[]{:T(128)S(6)} %add.335), channel_id=1, replica_groups=mesh['hours'=64,'region'=8] {'hours','region'}, use_global_device_ids=true, to_apply=%region_24.25 | all-reduce | flops 2 | bytes 16 | tf_op jit(solution)/shard_map/psum | solution.py:164
  1003.9 24.8 %all_gather.25 = f32[64,1024]{1,0:T(8,128)S(1)} all-gather(f32[64,128]{1,0:T(8,128)S(1)} %get-tuple-element.63), channel_id=1, replica_groups=mesh['hours'=64,'region'=8] {'region'}, dimensions={1}, use_global_device_ids=true | all-gather | bytes 294912 | tf_op jit(solution)/shard_map/all_gather | solution.py:85
  1029.5 120.4 %all-reduce.2 = f32[2048]{0:T(1024)S(1)} all-reduce(f32[2048]{0:T(1024)S(1)} %subtract_dynamic-update-slice_fusion), channel_id=1, replica_groups=mesh['hours'=64,'region'=8] {'hours'}, use_global_device_ids=true, to_apply=%add.2 | all-reduce | flops 2048 | bytes 16384
  1149.9 11.8 gather_fusion.5
  1168.1 11.8 gather_fusion.6
  1180.2 131.1 %psum.79 = f32[2048]{0:T(1024)S(1)} all-reduce(f32[2048]{0:T(1024)S(1)} %gather_fusion.6), channel_id=1, replica_groups=mesh['hours'=64,'region'=8] {'hours'}, use_global_device_ids=true, to_apply=%region_48.49 | all-reduce | flops 2048 | bytes 16384 | tf_op jit(solution)/shard_map/psum | solution.py:22
  1321.9 100.9 %all-reduce.3 = (f32[]{:T(128)}, f32[]{:T(128)}) all-reduce(f32[]{:T(128)S(6)} %add.349, f32[]{:T(128)S(6)} %add.355), channel_id=1, replica_groups=mesh['hours'=64,'region'=8] {'hours','region'}, use_global_device_ids=true, to_apply=%region_39.40 | all-reduce | flops 2 | bytes 16 | tf_op jit(solution)/shard_map/psum | solution.py:164
  1424.3 24.8 %all_gather.27 = f32[64,1024]{1,0:T(8,128)S(1)} all-gather(f32[64,128]{1,0:T(8,128)S(1)} %get-tuple-element.70), channel_id=1, replica_groups=mesh['hours'=64,'region'=8] {'region'}, dimensions={1}, use_global_device_ids=true | all-gather | bytes 294912 | tf_op jit(solution)/shard_map/all_gather | solution.py:85
  1455.2 32.9 %reduce-scatter.11.cloned.1.call-done = f32[64,128]{1,0:T(8,128)} async-done(((f32[64,1024]{1,0:T(8,128)}), f32[64,128]{1,0:T(8,128)}) %reduce-scatter.11.cloned.1.call-update) | async-done | bytes 32784 | tf_op jit(solution)/shard_map/reduce_scatter | solution.py:144
  (126 shorter events, 52.3 us)
Async XLA Ops:
  7.2 465.0 %reduce-scatter.5.cloned.1.call-start = ((), (), s32[]{:S(2)}) async-start(), calls=%async_computation.4 | async-start | bytes 294912 | tf_op jit(solution)/shard_map/reduce_scatter | solution.py:144
  7.9 2.1 copy-start.9
  7.9 461.4 %collective-permute-start = (f32[1,256]{1,0:T(1,128)S(1)}, f32[1,256]{1,0:T(1,128)S(1)}, u32[]{:S(2)}, u32[]{:S(2)}) collective-permute-start(f32[1,256]{1,0:T(1,128)S(1)} %bitcast.122), channel_id=1, source_target_pairs={{0,8},{8,16},{16,24},{24,32},{32,40},{40,48},{48,56},{56,64},{64,7... | collective-permute-start | bytes 3080 | tf_op jit(solution)/shard_map/ppermute | solution.py:14
  36.6 0.7 copy-start.13
  36.6 0.7 copy-start.12
  37.2 0.8 copy-start.1
  37.3 3.8 copy-start
  40.3 853.9 %reduce-scatter.7.cloned.1.call-start = ((), (), s32[]{:S(2)}) async-start(), calls=%async_computation.5 | async-start | bytes 294912 | tf_op jit(solution)/shard_map/reduce_scatter | solution.py:144
  40.3 0.7 copy-start.11
  40.3 0.7 copy-start.5
  40.4 0.7 copy-start.10
  181.0 0.7 copy-start.8
  314.0 11.8 copy-start.3
  340.6 126.1 %copy-start.7 = (f32[256]{0:T(256)S(1)}, f32[256]{0:T(256)}, u32[]{:S(2)}) copy-start(f32[256]{0:T(256)} %param.26) | copy-start | bytes 3076
  469.2 0.7 copy-start.4
  472.1 1.1 copy-start.2
  476.0 262.6 %collective-permute-start.1 = (f32[1,256]{1,0:T(1,128)S(1)}, f32[1,256]{1,0:T(1,128)S(1)}, u32[]{:S(2)}, u32[]{:S(2)}) collective-permute-start(f32[1,256]{1,0:T(1,128)S(1)} %slice.79), channel_id=1, source_target_pairs={{0,504},{8,0},{16,8},{24,16},{32,24},{40,32},{48,40},{56,48},{64,5... | collective-permute-start | bytes 3080 | tf_op jit(solution)/shard_map/ppermute | solution.py:14
  738.6 0.7 copy-start.6
  742.9 573.2 %reduce-scatter.9.cloned.1.call-start = ((), (), s32[]{:S(2)}) async-start(), calls=%async_computation.6 | async-start | bytes 294912 | tf_op jit(solution)/shard_map/reduce_scatter | solution.py:144
  756.0 135.9 %collective-permute-start.2 = (f32[1,256]{1,0:T(1,128)S(1)}, f32[1,256]{1,0:T(1,128)S(1)}, u32[]{:S(2)}, u32[]{:S(2)}) collective-permute-start(f32[1,256]{1,0:T(1,128)S(1)} %slice.80), channel_id=1, source_target_pairs={{0,8},{8,16},{16,24},{24,32},{32,40},{40,48},{48,56},{56,64},{64,7... | collective-permute-start | bytes 3080 | tf_op jit(solution)/shard_map/ppermute | solution.py:14
  898.0 130.7 %collective-permute-start.3 = (f32[1,256]{1,0:T(1,128)S(1)}, f32[1,256]{1,0:T(1,128)S(1)}, u32[]{:S(2)}, u32[]{:S(2)}) collective-permute-start(f32[1,256]{1,0:T(1,128)S(1)} %slice.83), channel_id=1, source_target_pairs={{0,504},{8,0},{16,8},{24,16},{32,24},{40,32},{48,40},{56,48},{64,5... | collective-permute-start | bytes 3080 | tf_op jit(solution)/shard_map/ppermute | solution.py:14
  1161.7 152.2 %collective-permute-start.4 = (f32[1,256]{1,0:T(1,128)S(1)}, f32[1,256]{1,0:T(1,128)S(1)}, u32[]{:S(2)}, u32[]{:S(2)}) collective-permute-start(f32[1,256]{1,0:T(1,128)S(1)} %slice.84), channel_id=1, source_target_pairs={{0,8},{8,16},{16,24},{24,32},{32,40},{40,48},{48,56},{56,64},{64,7... | collective-permute-start | bytes 3080 | tf_op jit(solution)/shard_map/ppermute | solution.py:14
  1166.6 321.5 %reduce-scatter.11.cloned.1.call-start = ((), (), s32[]{:S(2)}) async-start(), calls=%async_computation.7 | async-start | bytes 294912 | tf_op jit(solution)/shard_map/reduce_scatter | solution.py:144
  1320.0 134.3 %collective-permute-start.5 = (f32[1,256]{1,0:T(1,128)S(1)}, f32[1,256]{1,0:T(1,128)S(1)}, u32[]{:S(2)}, u32[]{:S(2)}) collective-permute-start(f32[1,256]{1,0:T(1,128)S(1)} %slice.87), channel_id=1, source_target_pairs={{0,504},{8,0},{16,8},{24,16},{32,24},{40,32},{48,40},{56,48},{64,5... | collective-permute-start | bytes 3080 | tf_op jit(solution)/shard_map/ppermute | solution.py:14
Sparse Core Ops, SparseCore 0:
  40.4 42.1 reduce-scatter.4
  743.0 39.1 reduce-scatter.6
  1166.7 41.5 reduce-scatter.8
  1453.5 34.5 reduce-scatter.10
where the time goes:
time: 1500 us
  blocking collectives  1280 us (85%)
  local copies, waits for them, and re-layouts  86.5 us (6%)
  between operations  36.6 us (2%)
  waiting for transfers between devices  33 us (2%)
  matrix products  26.5 us (2%)
  starting transfers between devices  16.8 us (1%)
  other arithmetic  16.8 us (1%)
    psum x4, blocking collectives, to_owners(): summed = lax.psum(partial_value, 'hours')  515 us
    unnamed x3, blocking collectives  367 us
    psum x3, blocking collectives, body(): dual_sum = lax.psum(dual_sq, ('hours', 'region'))  297 us
    all_gather x4, blocking collectives, body(): lax.all_gather(prices, 'region', axis=1, tiled=True)  101 us
    gather x3, local copies, waits for them, and re-layouts, body(): cap_dense = capacity_all[inverse].reshape(tech_count, node_count)  35.3 us
    gather x3, local copies, waits for them, and re-layouts, body(): jnp.sum(availability * cap_duals, axis=0).reshape(-1)[owner_cols]  35.3 us
    reduce_scatter x4, waiting for transfers between devices, body(): lax.psum_scatter(per_dest, 'region', scatter_dimension=1, tiled=True)  32.9 us
  transfers between devices with their start and end apart: 10, of which 1 were waited for; matrix products, arithmetic and copies ran while one was open for 7% of the time, Pallas kernels for 0%

commit v1 on v0

--- a/solution.py
+++ b/solution.py
@@ -161,7 +161,7 @@
                 + jnp.sum((cap_new - cap_duals) ** 2)
                 + jnp.sum((store_new - store_duals) ** 2)
             )
-            dual_sum = lax.psum(dual_sq, ("hours", "region"))
+            dual_sum = lax.psum(lax.psum(dual_sq, "region"), "hours")
             weight = jnp.sqrt(weight * jnp.sqrt((dual_sum + epsilon) / (primal_sum + epsilon)))
         dispatch, capacity, inner_flow, cross_flow = (
             dispatch_new,

time: 1500 us -> 1570 us (1.047)
  blocking collectives: 1280 us -> 1320 us
  waiting for transfers between devices: 33 us -> 59.9 us
    psum x3 -> x7, blocking collectives: 297 us -> 467 us  [the longest x3 292 us: body(): primal_sum = lax.psum(primal_sq, ('hours', 'region'))]
    psum x4 -> x3, blocking collectives: 515 us -> 373 us  [to_owners(): summed = lax.psum(partial_value, 'hours')]
    reduce_scatter x4, waiting for transfers between devices: 32.9 us -> 59.8 us  [body(): lax.psum_scatter(per_dest, 'region', scatter_dimension=1, tiled=True)]
  transfers between devices with their start and end apart: 10 -> 10, of which waited for: 1 -> 2; matrix products, arithmetic and copies ran while one was open for 7% -> 7% of each run, Pallas kernels for 0% -> 0%
where the time goes in v1:
time: 1570 us
  blocking collectives  1320 us (84%)
  local copies, waits for them, and re-layouts  86.5 us (6%)
  waiting for transfers between devices  59.9 us (4%)
  between operations  36.5 us (2%)
  matrix products  26.5 us (2%)
  starting transfers between devices  21.5 us (1%)
  other arithmetic  16.8 us (1%)
    unnamed x3, blocking collectives  379 us
    psum x3, blocking collectives, to_owners(): summed = lax.psum(partial_value, 'hours')  373 us
    psum x3, blocking collectives, body(): primal_sum = lax.psum(primal_sq, ('hours', 'region'))  292 us
    psum x4, blocking collectives, body(): dual_sum = lax.psum(lax.psum(dual_sq, 'region'), 'hours')  175 us
    all_gather x4, blocking collectives, body(): lax.all_gather(prices, 'region', axis=1, tiled=True)  101 us
    reduce_scatter x4, waiting for transfers between devices, body(): lax.psum_scatter(per_dest, 'region', scatter_dimension=1, tiled=True)  59.8 us
    gather x3, local copies, waits for them, and re-layouts, body(): cap_dense = capacity_all[inverse].reshape(tech_count, node_count)  35.3 us
    gather x3, local copies, waits for them, and re-layouts, body(): jnp.sum(availability * cap_duals, axis=0).reshape(-1)[owner_cols]  35.3 us
  transfers between devices with their start and end apart: 10, of which 2 were waited for; matrix products, arithmetic and copies ran while one was open for 7% of the time, Pallas kernels for 0%

profile of v1, /device:TPU:2, one launch (start us, length us, event | category | flops | bytes accessed | tf_op | source)
XLA Modules:
  0.0 1567.2 jit_solution(8037426835049234256)
XLA Ops:
  10.0 26.6 %all_gather.21 = f32[64,1024]{1,0:T(8,128)S(1)} all-gather(f32[64,128]{1,0:T(8,128)} %param.27), channel_id=1, replica_groups=mesh['hours'=64,'region'=8] {'region'}, dimensions={1}, use_global_device_ids=true | all-gather | bytes 294912 | tf_op jit(solution)/shard_map/all_gather | solution.py:85
  41.2 11.8 gather_fusion
  53.0 126.8 %psum.91 = f32[2048]{0:T(1024)S(1)} all-reduce(f32[2048]{0:T(1024)S(1)} %gather_fusion), channel_id=1, replica_groups=mesh['hours'=64,'region'=8] {'hours'}, use_global_device_ids=true, to_apply=%region_5.6 | all-reduce | flops 2048 | bytes 16384 | tf_op jit(solution)/shard_map/psum | solution.py:22
  182.5 126.4 %all-reduce = f32[2048]{0:T(1024)S(1)} all-reduce(f32[2048]{0:T(1024)S(1)} %multiply_dynamic-update-slice_fusion), channel_id=1, replica_groups=mesh['hours'=64,'region'=8] {'hours'}, use_global_device_ids=true, to_apply=%add | all-reduce | flops 2048 | bytes 16384
  352.6 95.6 %psum.94 = f32[]{:T(128)} all-reduce(f32[]{:T(128)S(6)} %add.321), channel_id=1, replica_groups=mesh['hours'=64,'region'=8] {'hours','region'}, use_global_device_ids=true, to_apply=%region_17.18 | all-reduce | flops 1 | bytes 8 | tf_op jit(solution)/shard_map/psum | solution.py:130
  452.7 17.2 %psum.92 = f32[]{:T(128)} all-reduce(f32[]{:T(128)S(6)} %add.315), channel_id=1, replica_groups=mesh['hours'=64,'region'=8] {'region'}, use_global_device_ids=true, to_apply=%region_9.10 | all-reduce | flops 1 | bytes 8 | tf_op jit(solution)/shard_map/psum | solution.py:164
  469.9 122.9 %all-reduce.5 = (f32[2048]{0:T(1024)S(1)}, f32[]{:T(128)}) all-reduce(f32[2048]{0:T(1024)S(1)} %gather_fusion.2, f32[]{:T(128)} %psum.92), channel_id=1, replica_groups=mesh['hours'=64,'region'=8] {'hours'}, use_global_device_ids=true, to_apply=%region_22.23 | all-reduce | flops 2049 | bytes 16392 | tf_op jit(solution)/shard_map/psum | solution.py:22
  593.6 25.0 %all_gather.23 = f32[64,1024]{1,0:T(8,128)S(1)} all-gather(f32[64,128]{1,0:T(8,128)S(1)} %get-tuple-element.56), channel_id=1, replica_groups=mesh['hours'=64,'region'=8] {'region'}, dimensions={1}, use_global_device_ids=true | all-gather | bytes 294912 | tf_op jit(solution)/shard_map/all_gather | solution.py:85
  620.4 126.1 %all-reduce.1 = f32[2048]{0:T(1024)S(1)} all-reduce(f32[2048]{0:T(1024)S(1)} %subtract_dynamic-update-slice_fusion.1), channel_id=1, replica_groups=mesh['hours'=64,'region'=8] {'hours'}, use_global_device_ids=true, to_apply=%add.1 | all-reduce | flops 2048 | bytes 16384
  746.5 11.8 gather_fusion.3
  766.2 11.8 gather_fusion.4
  789.7 98.2 %psum.98 = f32[]{:T(128)} all-reduce(f32[]{:T(128)S(6)} %add.341), channel_id=1, replica_groups=mesh['hours'=64,'region'=8] {'hours','region'}, use_global_device_ids=true, to_apply=%region_33.34 | all-reduce | flops 1 | bytes 8 | tf_op jit(solution)/shard_map/psum | solution.py:130
  892.4 17.3 %psum.96 = f32[]{:T(128)} all-reduce(f32[]{:T(128)S(6)} %add.335), channel_id=1, replica_groups=mesh['hours'=64,'region'=8] {'region'}, use_global_device_ids=true, to_apply=%region_25.26 | all-reduce | flops 1 | bytes 8 | tf_op jit(solution)/shard_map/psum | solution.py:164
  909.7 122.9 %all-reduce.4 = (f32[2048]{0:T(1024)S(1)}, f32[]{:T(128)}) all-reduce(f32[2048]{0:T(1024)S(1)} %gather_fusion.4, f32[]{:T(128)} %psum.96), channel_id=1, replica_groups=mesh['hours'=64,'region'=8] {'hours'}, use_global_device_ids=true, to_apply=%region_38.39 | all-reduce | flops 2049 | bytes 16392 | tf_op jit(solution)/shard_map/psum | solution.py:22
  1035.2 24.8 %all_gather.25 = f32[64,1024]{1,0:T(8,128)S(1)} all-gather(f32[64,128]{1,0:T(8,128)S(1)} %get-tuple-element.63), channel_id=1, replica_groups=mesh['hours'=64,'region'=8] {'region'}, dimensions={1}, use_global_device_ids=true | all-gather | bytes 294912 | tf_op jit(solution)/shard_map/all_gather | solution.py:85
  1060.8 126.1 %all-reduce.2 = f32[2048]{0:T(1024)S(1)} all-reduce(f32[2048]{0:T(1024)S(1)} %subtract_dynamic-update-slice_fusion), channel_id=1, replica_groups=mesh['hours'=64,'region'=8] {'hours'}, use_global_device_ids=true, to_apply=%add.2 | all-reduce | flops 2048 | bytes 16384
  1187.0 11.8 gather_fusion.5
  1205.5 11.8 gather_fusion.6
  1222.0 22.1 %reduce-scatter.9.cloned.1.call-done = f32[64,128]{1,0:T(8,128)} async-done(((f32[64,1024]{1,0:T(8,128)}), f32[64,128]{1,0:T(8,128)}) %reduce-scatter.9.cloned.1.call-update) | async-done | bytes 32784 | tf_op jit(solution)/shard_map/reduce_scatter | solution.py:144
  1249.9 98.1 %psum.102 = f32[]{:T(128)} all-reduce(f32[]{:T(128)S(6)} %add.361), channel_id=1, replica_groups=mesh['hours'=64,'region'=8] {'hours','region'}, use_global_device_ids=true, to_apply=%region_49.50 | all-reduce | flops 1 | bytes 8 | tf_op jit(solution)/shard_map/psum | solution.py:130
  1348.0 16.5 %psum.100 = f32[]{:T(128)} all-reduce(f32[]{:T(128)S(6)} %add.355), channel_id=1, replica_groups=mesh['hours'=64,'region'=8] {'region'}, use_global_device_ids=true, to_apply=%region_41.42 | all-reduce | flops 1 | bytes 8 | tf_op jit(solution)/shard_map/psum | solution.py:164
  1365.1 124.2 %all-reduce.3 = (f32[]{:T(128)}, f32[2048]{0:T(1024)S(1)}) all-reduce(f32[]{:T(128)} %psum.100, f32[2048]{0:T(1024)S(1)} %gather_fusion.6), channel_id=1, replica_groups=mesh['hours'=64,'region'=8] {'hours'}, use_global_device_ids=true, to_apply=%region_42.43 | all-reduce | flops 2049 | bytes 16392 | tf_op jit(solution)/shard_map/psum | solution.py:164
  1490.1 24.9 %all_gather.27 = f32[64,1024]{1,0:T(8,128)S(1)} all-gather(f32[64,128]{1,0:T(8,128)S(1)} %get-tuple-element.70), channel_id=1, replica_groups=mesh['hours'=64,'region'=8] {'region'}, dimensions={1}, use_global_device_ids=true | all-gather | bytes 294912 | tf_op jit(solution)/shard_map/all_gather | solution.py:85
  1521.1 37.7 %reduce-scatter.11.cloned.1.call-done = f32[64,128]{1,0:T(8,128)} async-done(((f32[64,1024]{1,0:T(8,128)}), f32[64,128]{1,0:T(8,128)}) %reduce-scatter.11.cloned.1.call-update) | async-done | bytes 32784 | tf_op jit(solution)/shard_map/reduce_scatter | solution.py:144
  (129 shorter events, 92.5 us)
Async XLA Ops:
  7.2 441.1 %reduce-scatter.5.cloned.1.call-start = ((), (), s32[]{:S(2)}) async-start(), calls=%async_computation.4 | async-start | bytes 294912 | tf_op jit(solution)/shard_map/reduce_scatter | solution.py:144
  7.9 2.1 copy-start.9
  7.9 335.2 %collective-permute-start = (f32[1,256]{1,0:T(1,128)S(1)}, f32[1,256]{1,0:T(1,128)S(1)}, u32[]{:S(2)}, u32[]{:S(2)}) collective-permute-start(f32[1,256]{1,0:T(1,128)S(1)} %bitcast.122), channel_id=1, source_target_pairs={{0,8},{8,16},{16,24},{24,32},{32,40},{40,48},{48,56},{56,64},{64,7... | collective-permute-start | bytes 3080 | tf_op jit(solution)/shard_map/ppermute | solution.py:14
  36.6 0.7 copy-start.13
  36.6 0.7 copy-start.12
  37.2 0.8 copy-start.1
  37.3 3.8 copy-start
  40.3 847.7 %reduce-scatter.7.cloned.1.call-start = ((), (), s32[]{:S(2)}) async-start(), calls=%async_computation.5 | async-start | bytes 294912 | tf_op jit(solution)/shard_map/reduce_scatter | solution.py:144
  40.3 0.7 copy-start.11
  40.3 0.7 copy-start.5
  40.4 0.7 copy-start.10
  181.0 0.7 copy-start.8
  314.0 11.8 copy-start.3
  328.1 0.7 copy-start.7
  343.1 0.7 copy-start.4
  346.0 412.3 %collective-permute-start.1 = (f32[1,256]{1,0:T(1,128)S(1)}, f32[1,256]{1,0:T(1,128)S(1)}, u32[]{:S(2)}, u32[]{:S(2)}) collective-permute-start(f32[1,256]{1,0:T(1,128)S(1)} %slice.79), channel_id=1, source_target_pairs={{0,504},{8,0},{16,8},{24,16},{32,24},{40,32},{48,40},{56,48},{64,5... | collective-permute-start | bytes 3080 | tf_op jit(solution)/shard_map/ppermute | solution.py:14
  448.2 1.0 copy-start.2
  758.3 0.7 copy-start.6
  759.7 20.8 %collective-permute-start.2 = (f32[1,256]{1,0:T(1,128)S(1)}, f32[1,256]{1,0:T(1,128)S(1)}, u32[]{:S(2)}, u32[]{:S(2)}) collective-permute-start(f32[1,256]{1,0:T(1,128)S(1)} %slice.80), channel_id=1, source_target_pairs={{0,8},{8,16},{16,24},{24,32},{32,40},{40,48},{48,56},{56,64},{64,7... | collective-permute-start | bytes 3080 | tf_op jit(solution)/shard_map/ppermute | solution.py:14
  764.6 479.5 %reduce-scatter.9.cloned.1.call-start = ((), (), s32[]{:S(2)}) async-start(), calls=%async_computation.6 | async-start | bytes 294912 | tf_op jit(solution)/shard_map/reduce_scatter | solution.py:144
  782.8 277.3 %collective-permute-start.3 = (f32[1,256]{1,0:T(1,128)S(1)}, f32[1,256]{1,0:T(1,128)S(1)}, u32[]{:S(2)}, u32[]{:S(2)}) collective-permute-start(f32[1,256]{1,0:T(1,128)S(1)} %slice.83), channel_id=1, source_target_pairs={{0,504},{8,0},{16,8},{24,16},{32,24},{40,32},{48,40},{56,48},{64,5... | collective-permute-start | bytes 3080 | tf_op jit(solution)/shard_map/ppermute | solution.py:14
  1198.8 21.0 %collective-permute-start.4 = (f32[1,256]{1,0:T(1,128)S(1)}, f32[1,256]{1,0:T(1,128)S(1)}, u32[]{:S(2)}, u32[]{:S(2)}) collective-permute-start(f32[1,256]{1,0:T(1,128)S(1)} %slice.84), channel_id=1, source_target_pairs={{0,8},{8,16},{16,24},{24,32},{32,40},{40,48},{48,56},{56,64},{64,7... | collective-permute-start | bytes 3080 | tf_op jit(solution)/shard_map/ppermute | solution.py:14
  1203.7 355.2 %reduce-scatter.11.cloned.1.call-start = ((), (), s32[]{:S(2)}) async-start(), calls=%async_computation.7 | async-start | bytes 294912 | tf_op jit(solution)/shard_map/reduce_scatter | solution.py:144
  1247.9 272.3 %collective-permute-start.5 = (f32[1,256]{1,0:T(1,128)S(1)}, f32[1,256]{1,0:T(1,128)S(1)}, u32[]{:S(2)}, u32[]{:S(2)}) collective-permute-start(f32[1,256]{1,0:T(1,128)S(1)} %slice.87), channel_id=1, source_target_pairs={{0,504},{8,0},{16,8},{24,16},{32,24},{40,32},{48,40},{56,48},{64,5... | collective-permute-start | bytes 3080 | tf_op jit(solution)/shard_map/ppermute | solution.py:14
Sparse Core Ops, SparseCore 0:
  40.4 42.1 reduce-scatter.4
  764.7 39.7 reduce-scatter.6
  1203.8 40.2 reduce-scatter.8
  1519.4 39.3 reduce-scatter.10
